TPU v7x, 32 devices: a whole 2x2x4 slice. The times are simulated.
32 devices in a mesh: dp: 8 (over z, core), mp: 4 (over y, x).
Axes of the slice: x: 2, y: 2, z: 4, core: 2. Of those that a mesh axis runs over, the one named last changes fastest.
Arguments:
- grads: bfloat16 [8192, 2048], P('mp', 'dp'), may hold values from -24 to 24
- old_factor: float32 [8192, 8192], P('mp', 'dp'), may hold values from -1 to 16, as said below
- basis: float32 [8192, 512], P('mp', 'dp'), may hold values from -6 to 6
Outputs:
- new_factor: float32 [8192, 8192], P('mp', 'dp')
- new_basis: float32 [8192, 512], P('mp', 'dp')
- basis_one: float32 [8192, 512], P('dp')
Inputs may be any that keep to these rules, and one draw needn't show every extreme that they name: old_factor is symmetric; its diagonal lies between 1 and 16 and its off-diagonal entries between -2.3/sqrt(8192) and 2.3/sqrt(8192).
All inputs are finite; a program needn't handle non-finite values.
Results may differ from a plain program's by a relative error of at most 0.0003.
Values may be sent and summed in bfloat16 or wider, within the bound.
A program may use at most 256 MiB of HBM per device.

v0:
```python
import jax
import jax.numpy as jnp
from jax import lax
from jax.sharding import PartitionSpec as P

D = 8192


def from_root(value, axis, root):
    mine = lax.axis_index(axis) == root
    return lax.psum(jnp.where(mine, value, jnp.zeros_like(value)), axis)


def contract_lead(left, right):
    return lax.dot_general(
        left,
        right,
        (((0,), (0,)), ((), ())),
        precision=lax.Precision.HIGHEST,
        preferred_element_type=jnp.float32,
    )


def contract_last(left, right):
    return lax.dot_general(
        left,
        right,
        (((1,), (1,)), ((), ())),
        precision=lax.Precision.HIGHEST,
        preferred_element_type=jnp.float32,
    )


def body(grads, old_factor, basis):
    cols_here = old_factor.shape[1]
    block_cols = grads.shape[1]
    num_mp = lax.axis_size("mp")
    num_dp = lax.axis_size("dp")
    total_cols = block_cols * num_dp
    basis_cols = basis.shape[1] * num_dp
    stripe_full = lax.all_gather(grads, "dp", axis=1, tiled=True)
    ratio = num_dp // num_mp
    offset = lax.axis_index("dp") % ratio * cols_here
    local_panel = lax.dynamic_slice_in_dim(stripe_full, offset, cols_here, 0)
    panel_full = from_root(local_panel, "mp", lax.axis_index("dp") // ratio)
    summed_block = lax.dot_general(
        stripe_full, panel_full, (((1,), (1,)), ((), ())), preferred_element_type=jnp.float32
    )
    new_factor = 0.95 * old_factor + 0.05 / total_cols * summed_block
    basis_full = lax.all_gather(basis, "dp", axis=1, tiled=True)
    product_one = lax.psum(contract_lead(basis_full, new_factor), "mp")
    gram_one = lax.psum(contract_last(product_one, product_one), "dp") / D
    lower_one = jnp.linalg.cholesky(gram_one)
    basis_one = lax.linalg.triangular_solve(lower_one, product_one, left_side=True, lower=True)
    product_two = lax.psum(contract_last(basis_one, new_factor), "dp")
    gram_two = lax.psum(contract_last(product_two, product_two), "mp") / D
    lower_two = jnp.linalg.cholesky(gram_two)
    basis_two = lax.linalg.triangular_solve(lower_two, product_two, left_side=True, lower=True)
    panel_width = basis_cols // num_dp
    own_rows = lax.dynamic_slice_in_dim(
        basis_two, lax.axis_index("dp") * panel_width, panel_width, 0
    )
    return (new_factor, own_rows.T, basis_one.T)


def solution(mesh):
    placed = (P("mp", "dp"), P("mp", "dp"), P("mp", "dp"))
    return jax.shard_map(
        body,
        mesh=mesh,
        in_specs=placed,
        out_specs=(P("mp", "dp"), P("mp", "dp"), P("dp", None)),
        check_vma=False,
    )
```

profile of v0, /device:TPU:0, one launch (start us, length us, event | category | flops | bytes accessed | tf_op | source)
XLA Modules:
  0.0 895.2 jit_solution(5238847923584072459)
XLA Ops:
  8.0 86.9 %all-gather.3.cloned.1.call-done = bf16[2048,2048]{1,0:T(8,128)(2,1)} async-done(((bf16[2048,256]{1,0:T(8,128)(2,1)}), bf16[2048,2048]{1,0:T(8,128)(2,1)}) %all-gather.3.cloned.1.call-update) | async-done | bytes 8388624 | tf_op jit(solution)/shard_map/all_gather | solution.py:41
  94.8 5.4 dynamic-slice_select_fusion
  101.1 9.2 %copy.6 = f32[2048,1024]{0,1:T(8,128)} copy(f32[2048,1024]{1,0:T(8,128)} %param.5) | data formatting | bytes 16777216 | tf_op args[1]
  110.3 92.2 %all-reduce.7.cloned.1.call-done = bf16[1024,2048]{1,0:T(8,128)(2,1)} async-done(((bf16[1024,2048]{1,0:T(8,128)(2,1)}), bf16[1024,2048]{1,0:T(8,128)(2,1)}) %all-reduce.7.cloned.1.call-update) | async-done | bytes 4194320 | tf_op jit(solution)/shard_map/psum | solution.py:11
  202.5 15.9 %bitcast_add_fusion = f32[2048,1024]{0,1:T(8,128)} fusion(f32[2048,1024]{0,1:T(8,128)} %copy.6, bf16[1024,2048]{1,0:T(8,128)(2,1)} %all-reduce.7.cloned.1.call-done, bf16[2048,2048]{1,0:T(8,128)(2,1)} %all-gather.3.cloned.1.call-done), kind=kOutput, calls=%fused_computation.4 | convolution fusion | flops 8596226048 | bytes 29360128 | tf_op jit(solution)/shard_map/dot_general | solution.py:46
  218.4 32.9 %all-gather.5.cloned.1.call-done = f32[2048,512]{0,1:T(8,128)} async-done(((f32[2048,64]{0,1:T(8,128)}), f32[2048,512]{0,1:T(8,128)}) %all-gather.5.cloned.1.call-update) | async-done | bytes 4194320 | tf_op jit(solution)/shard_map/all_gather | solution.py:50
  251.3 17.1 %convolution_bitcast_fusion = f32[512,1024]{0,1:T(8,128)} fusion(f32[2048,1024]{0,1:T(8,128)} %bitcast_add_fusion, f32[2048,512]{0,1:T(8,128)} %all-gather.5.cloned.1.call-done), kind=kOutput, calls=%fused_computation.23 | convolution fusion | flops 12884901888 | bytes 14680064 | tf_op jit(solution)/shard_map/dot_general | solution.py:15
  268.8 68.2 %all-reduce.9.cloned.1.call-done = f32[512,1024]{0,1:T(8,128)} async-done(((f32[512,1024]{0,1:T(8,128)}), f32[512,1024]{0,1:T(8,128)}) %all-reduce.9.cloned.1.call-update) | async-done | bytes 2097168 | tf_op jit(solution)/shard_map/psum | solution.py:51
  337.0 6.8 fusion.85
  343.8 58.9 %all-reduce.11.cloned.1.call-done = f32[512,512]{0,1:T(8,128)} async-done(((f32[512,512]{0,1:T(8,128)}), f32[512,512]{0,1:T(8,128)}) %all-reduce.11.cloned.1.call-update) | async-done | bytes 1048592 | tf_op jit(solution)/shard_map/psum | solution.py:52
  402.7 1.4 broadcast_multiply_fusion.1
  404.7 1.0 copy-done.5
  405.7 11.7 %cholesky.286 = f32[128,128]{1,0:T(8,128)S(1)} custom-call(f32[128,128]{1,0:T(8,128)S(1)} %cholesky.426), custom_call_target="Cholesky" | custom-call | tf_op jit(solution)/shard_map/jit(cholesky)/cholesky | solution.py:53
  417.6 9.8 %custom-call.31 = f32[1,128,128]{1,2,0:T(8,128)S(1)} custom-call(f32[1,128,128]{2,1,0:T(8,128)S(1)} %get-tuple-element.62), custom_call_target="InvertDiagBlocksLowerTriangular" | custom-call | tf_op jit(solution)/shard_map/jit(cholesky)/cholesky | solution.py:53
  427.4 1.2 constant_dynamic-update-slice_fusion.3
  428.6 1.3 convolution_subtract_fusion.5
  429.9 11.7 %cholesky.305 = f32[128,128]{1,0:T(8,128)S(1)} custom-call(f32[128,128]{1,0:T(8,128)S(1)} %cholesky.430), custom_call_target="Cholesky" | custom-call | tf_op jit(solution)/shard_map/jit(cholesky)/cholesky | solution.py:53
  441.7 18.5 %custom-call.32 = f32[1,128,128]{1,2,0:T(8,128)S(1)} custom-call(f32[1,128,128]{2,1,0:T(8,128)S(1)} %get-tuple-element.59), custom_call_target="InvertDiagBlocksLowerTriangular" | custom-call | tf_op jit(solution)/shard_map/jit(cholesky)/cholesky | solution.py:53
  460.5 1.3 convolution_subtract_fusion.7
  461.8 11.7 %cholesky.326 = f32[128,128]{1,0:T(8,128)S(1)} custom-call(f32[128,128]{1,0:T(8,128)S(1)} %cholesky.435), custom_call_target="Cholesky" | custom-call | tf_op jit(solution)/shard_map/jit(cholesky)/cholesky | solution.py:53
  474.2 9.8 %custom-call.33 = f32[1,128,128]{1,2,0:T(8,128)S(1)} custom-call(f32[1,128,128]{2,1,0:T(8,128)S(1)} %get-tuple-element.56), custom_call_target="InvertDiagBlocksLowerTriangular" | custom-call | tf_op jit(solution)/shard_map/jit(cholesky)/cholesky | solution.py:53
  484.2 1.2 convolution_subtract_fusion.9
  485.5 11.7 %cholesky.343 = f32[128,128]{1,0:T(8,128)S(1)} custom-call(f32[128,128]{1,0:T(8,128)S(1)} %convolution_subtract_fusion.9), custom_call_target="Cholesky" | custom-call | tf_op jit(solution)/shard_map/jit(cholesky)/cholesky | solution.py:53
  497.8 0.8 compare_reduce_fusion.6
  501.2 1.1 select_select_fusion.1
  502.3 11.9 %while.2 = (s32[]{:T(128)}, f32[512,512]{1,0:T(8,128)}, s32[4,2]{0,1:T(2,128)S(1)}, f32[4,128,128]{2,1,0:T(8,128)S(1)}, s32[]{:T(128)}) while((s32[]{:T(128)}, f32[512,512]{1,0:T(8,128)}, s32[4,2]{0,1:T(2,128)S(1)}, f32[4,128,128]{2,1,0:T(8,128)S(1)}, s32[]{:T(128)}) %tuple.54), condition=%wide.while_cond, body=%wide.while_body.sunk | while | flops 2 | bytes 131181 | solution.py:54
  503.0 2.3 bitcast_dynamic-update-slice_fusion.4
  506.0 2.3 bitcast_dynamic-update-slice_fusion.4
  508.9 2.3 bitcast_dynamic-update-slice_fusion.4
  511.9 2.3 bitcast_dynamic-update-slice_fusion.4
  514.2 39.3 %custom-call.26 = f32[4,128,128]{1,2,0:T(8,128)S(1)} custom-call(f32[4,128,128]{2,1,0:T(8,128)S(1)} %get-tuple-element.11), custom_call_target="InvertDiagBlocksLowerTriangular" | custom-call | tf_op jit(solution)/shard_map/triangular_solve | solution.py:54
  554.2 1.8 convolution_subtract_fusion.3
  556.7 2.7 convolution_subtract_fusion.2
  560.0 3.8 fusion.18
  565.3 17.7 %fusion.22 = f32[512,2048]{1,0:T(8,128)} fusion(f32[2048,1024]{0,1:T(8,128)} %bitcast_add_fusion, f32[128,1024]{1,0:T(8,128)S(1)} %fusion.58, f32[128,1024]{1,0:T(8,128)S(1)} %fusion.59, f32[128,1024]{1,0:T(8,128)S(1)} %fusion.61, f32[128,1024]{1,0:T(8,128)S(1)} %fusion.34), kind=kOutput, calls=%fused_computation.34 | convolution fusion | flops 12886474752 | bytes 14680064 | tf_op jit(solution)/shard_map/dot_general | solution.py:25
  583.1 95.6 %all-reduce.13.cloned.1.call-done = f32[512,2048]{1,0:T(8,128)} async-done(((f32[512,2048]{1,0:T(8,128)}), f32[512,2048]{1,0:T(8,128)}) %all-reduce.13.cloned.1.call-update) | async-done | bytes 4194320 | tf_op jit(solution)/shard_map/psum | solution.py:55
  678.6 10.2 %fusion.86 = f32[512,512]{0,1:T(8,128)} fusion(f32[512,2048]{1,0:T(8,128)} %all-reduce.13.cloned.1.call-done), kind=kOutput, calls=%fused_computation.152 | convolution fusion | flops 6442450944 | bytes 5242880 | tf_op jit(solution)/shard_map/dot_general | solution.py:25
  688.9 9.3 %copy.11 = f32[2048,1024]{1,0:T(8,128)} copy(f32[2048,1024]{0,1:T(8,128)} %bitcast_add_fusion) | data formatting | bytes 16777216
  698.1 1.4 fusion.21
  699.5 2.0 copy.12
  701.5 40.1 %all-reduce.15.cloned.1.call-done = f32[512,512]{0,1:T(8,128)} async-done(((f32[512,512]{0,1:T(8,128)}), f32[512,512]{0,1:T(8,128)}) %all-reduce.15.cloned.1.call-update) | async-done | bytes 1048592 | tf_op jit(solution)/shard_map/psum | solution.py:56
  741.6 1.4 broadcast_multiply_fusion
  743.7 11.7 %cholesky.358 = f32[128,128]{1,0:T(8,128)S(1)} custom-call(f32[128,128]{1,0:T(8,128)S(1)} %cholesky.439), custom_call_target="Cholesky" | custom-call | tf_op jit(solution)/shard_map/jit(cholesky)/cholesky | solution.py:57
  755.5 9.8 %custom-call.34 = f32[1,128,128]{1,2,0:T(8,128)S(1)} custom-call(f32[1,128,128]{2,1,0:T(8,128)S(1)} %get-tuple-element.52), custom_call_target="InvertDiagBlocksLowerTriangular" | custom-call | tf_op jit(solution)/shard_map/jit(cholesky)/cholesky | solution.py:57
  766.0 11.7 %cholesky.377 = f32[128,128]{1,0:T(8,128)S(1)} custom-call(f32[128,128]{1,0:T(8,128)S(1)} %cholesky.443), custom_call_target="Cholesky" | custom-call | tf_op jit(solution)/shard_map/jit(cholesky)/cholesky | solution.py:57
  779.1 10.0 %custom-call.35 = f32[1,128,128]{1,2,0:T(8,128)S(1)} custom-call(f32[1,128,128]{2,1,0:T(8,128)S(1)} %get-tuple-element.49), custom_call_target="InvertDiagBlocksLowerTriangular" | custom-call | tf_op jit(solution)/shard_map/jit(cholesky)/cholesky | solution.py:57
  789.8 11.7 %cholesky.398 = f32[128,128]{1,0:T(8,128)S(1)} custom-call(f32[128,128]{1,0:T(8,128)S(1)} %cholesky.448), custom_call_target="Cholesky" | custom-call | tf_op jit(solution)/shard_map/jit(cholesky)/cholesky | solution.py:57
  802.2 9.8 %custom-call.36 = f32[1,128,128]{1,2,0:T(8,128)S(1)} custom-call(f32[1,128,128]{2,1,0:T(8,128)S(1)} %get-tuple-element.46), custom_call_target="InvertDiagBlocksLowerTriangular" | custom-call | tf_op jit(solution)/shard_map/jit(cholesky)/cholesky | solution.py:57
  812.6 11.7 %cholesky.415 = f32[128,128]{1,0:T(8,128)S(1)} custom-call(f32[128,128]{1,0:T(8,128)S(1)} %convolution_subtract_fusion.8), custom_call_target="Cholesky" | custom-call | tf_op jit(solution)/shard_map/jit(cholesky)/cholesky | solution.py:57
  824.3 0.9 compare_reduce_fusion
  827.9 8.5 while.3
  828.6 1.4 bitcast_dynamic-update-slice_fusion.5
  830.7 1.4 bitcast_dynamic-update-slice_fusion.5
  832.9 1.4 bitcast_dynamic-update-slice_fusion.5
  835.0 1.4 bitcast_dynamic-update-slice_fusion.5
  836.4 39.3 %custom-call.27 = f32[4,128,128]{1,2,0:T(8,128)S(1)} custom-call(f32[4,128,128]{2,1,0:T(8,128)S(1)} %get-tuple-element.19), custom_call_target="InvertDiagBlocksLowerTriangular" | custom-call | tf_op jit(solution)/shard_map/triangular_solve | solution.py:58
  875.8 2.4 fusion.23
  878.2 2.2 convolution_subtract_fusion.1
  880.4 1.1 fusion.55
  881.5 1.3 convolution_subtract_fusion
  882.8 1.1 fusion.53
  883.8 2.0 fusion.6
  885.9 1.0 fusion.52
  886.9 1.0 fusion.33
  (85 shorter events, 18.1 us)
Async XLA Ops:
  7.2 87.7 %all-gather.3.cloned.1.call-start = ((), (), s32[]{:S(2)}) async-start(), calls=%async_computation | async-start | bytes 9437184 | tf_op jit(solution)/shard_map/all_gather | solution.py:41
  7.9 194.6 %all-reduce.7.cloned.1.call-start = ((), (), s32[]{:S(2)}) async-start(), calls=%async_computation.1 | async-start | bytes 8388608 | tf_op jit(solution)/shard_map/psum | solution.py:11
  100.3 151.1 %all-gather.5.cloned.1.call-start = ((), (), s32[]{:S(2)}) async-start(), calls=%async_computation.2 | async-start | bytes 4718592 | tf_op jit(solution)/shard_map/all_gather | solution.py:50
  101.0 236.0 %all-reduce.9.cloned.1.call-start = ((), (), s32[]{:S(2)}) async-start(), calls=%async_computation.3 | async-start | bytes 4194304 | tf_op jit(solution)/shard_map/psum | solution.py:51
  268.4 134.3 %all-reduce.11.cloned.1.call-start = ((), (), s32[]{:S(2)}) async-start(), calls=%async_computation.4 | async-start | bytes 2097152 | tf_op jit(solution)/shard_map/psum | solution.py:52
  343.8 334.9 %all-reduce.13.cloned.1.call-start = ((), (), s32[]{:S(2)}) async-start(), calls=%async_computation.5 | async-start | bytes 8388608 | tf_op jit(solution)/shard_map/psum | solution.py:55
  402.7 1.8 copy-start.4
  404.7 1.0 copy-start.5
  405.7 147.8 %copy-start.1 = (f32[512,1024]{0,1:T(8,128)S(1)}, f32[512,1024]{0,1:T(8,128)}, u32[]{:S(2)}) copy-start(f32[512,1024]{0,1:T(8,128)} %all-reduce.9.cloned.1.call-done) | copy-start | bytes 6291460
  560.0 4.5 copy-start.2
  564.5 0.8 copy-start.6
  583.0 158.6 %all-reduce.15.cloned.1.call-start = ((), (), s32[]{:S(2)}) async-start(), calls=%async_computation.6 | async-start | bytes 2097152 | tf_op jit(solution)/shard_map/psum | solution.py:56
  741.6 1.8 copy-start.3
  875.7 5.7 copy-start
Sparse Core Ops, SparseCore 0:
  9.6 85.1 all-gather.2
  100.4 102.0 all-reduce.6
  204.2 47.1 all-gather.4
  268.6 68.3 all-reduce.8
  343.9 58.7 all-reduce.10
  583.2 95.4 all-reduce.12
  689.0 52.5 all-reduce.14
where the time goes:
time: 903 us; the launch traced here: 895 us
  waiting for transfers between devices  476 us (53%)
  other arithmetic  258 us (29%)
  matrix products  97 us (11%)
  local copies, waits for them, and re-layouts  43.4 us (5%)
  between operations  20.1 us (2%)
    psum x1, waiting for transfers between devices, body(): product_two = lax.psum(contract_last(basis_one, new_factor), 'dp')  95.6 us
    psum x1, waiting for transfers between devices, from_root(): return lax.psum(jnp.where(mine, value, jnp.zeros_like(value)), axis)  92.2 us
    another operation x14, other arithmetic, body(): lower_one = jnp.linalg.cholesky(gram_one)  87.3 us
    all_gather x1, waiting for transfers between devices, body(): stripe_full = lax.all_gather(grads, 'dp', axis=1, tiled=True)  86.9 us
    another operation x15, other arithmetic, body(): lower_two = jnp.linalg.cholesky(gram_two)  79.5 us
    psum x1, waiting for transfers between devices, body(): product_one = lax.psum(contract_lead(basis_full, new_factor), 'mp')  68.2 us
    psum x1, waiting for transfers between devices, body(): gram_one = lax.psum(contract_last(product_one, product_one), 'dp') / D  58.9 us
    another operation x3, other arithmetic, body(): lax.linalg.triangular_solve(lower_one, product_one, left_side=True, lower...  40.4 us
  transfers between devices with their start and end apart: 7, of which 7 were waited for; matrix products, arithmetic and copies ran while one was open for 4% of the time, Pallas kernels for 0%

commit v1 on v0

v1 whole, which is shorter than its diff:
```python
import functools

import jax
import jax.numpy as jnp
from jax import lax
from jax.experimental import pallas as pl
from jax.experimental.pallas import tpu as pltpu
from jax.sharding import PartitionSpec as P

D = 8192
MESH = pl.DeviceIdType.MESH
HIGHEST = lax.Precision.HIGHEST
BLOCK = 128
STEP = 8


def dot(left, right, dims, precision=HIGHEST):
    return lax.dot_general(
        left, right, (dims, ((), ())), precision=precision, preferred_element_type=jnp.float32
    )


def invert_block(block, step):
    n = block.shape[0]
    row_id = lax.broadcasted_iota(jnp.int32, (n, n), 0)
    col_id = lax.broadcasted_iota(jnp.int32, (n, n), 1)
    left = block
    right = jnp.where(row_id == col_id, 1.0, 0.0).astype(jnp.float32)
    done = []
    for k in range(0, n, step):
        low = k // 8 * 8
        if low + left.shape[0] > n:
            cut = low - (n - left.shape[0])
            done.append((right[:cut], pivots))
            left, right = left[cut:], right[cut:]
        if k % 8 == 0:
            pivots = jnp.zeros((8, n), jnp.float32)
        ids = row_id[low:]
        reps = [jnp.broadcast_to(left[:, k + p : k + p + 1], left.shape) for p in range(step)]
        for p in range(step):
            at = k + p - low
            pivots = jnp.where(row_id[:8] == at, reps[p][:8], pivots)
            inverse = 1.0 / reps[p][at : at + 1]
            mult = jnp.where(ids > k + p, reps[p] * inverse, 0.0)
            for q in range(p + 1, step):
                reps[q] = reps[q] - mult * reps[q][at : at + 1]
            left = left - mult * left[at : at + 1]
            right = right - mult * right[at : at + 1]
    done.append((right, pivots))
    return jnp.concatenate([r * lax.rsqrt(p) for r, p in done], axis=0)


def factor_kernel(gram_ref, out_ref, work):
    n = gram_ref.shape[0]
    work[...] = gram_ref[...]
    row_id = lax.broadcasted_iota(jnp.int32, (n, n), 0)
    col_id = lax.broadcasted_iota(jnp.int32, (n, n), 1)
    out_ref[...] = jnp.where(row_id == col_id, 1.0, 0.0).astype(jnp.float32)

    def body(b, carry):
        at = pl.multiple_of(b * BLOCK, BLOCK)
        inv = invert_block(work[pl.ds(at, BLOCK), pl.ds(at, BLOCK)], STEP)
        upper = dot(inv, work[pl.ds(at, BLOCK), :], ((1,), (0,)))
        side = dot(inv, out_ref[pl.ds(at, BLOCK), :], ((1,), (0,)))
        keep = lax.broadcasted_iota(jnp.int32, (BLOCK, n), 1) >= at + BLOCK
        below = jnp.where(keep, upper, 0.0)
        work[...] -= dot(below, upper, ((0,), (0,)))
        out_ref[...] -= dot(below, side, ((0,), (0,)))
        out_ref[pl.ds(at, BLOCK), :] = side
        return carry

    lax.fori_loop(0, n // BLOCK, body, 0)


def inverse_factor(gram):
    return pl.pallas_call(
        factor_kernel,
        out_shape=jax.ShapeDtypeStruct(gram.shape, jnp.float32),
        in_specs=[pl.BlockSpec(memory_space=pltpu.VMEM)],
        out_specs=pl.BlockSpec(memory_space=pltpu.VMEM),
        scratch_shapes=[pltpu.VMEM(gram.shape, jnp.float32)],
        compiler_params=pltpu.CompilerParams(vmem_limit_bytes=40 * 2**20),
    )(gram)


def rows_at(index, size):
    return pl.ds(pl.multiple_of(index * size, size), size)


def place():
    dp, mp = lax.axis_index("dp"), lax.axis_index("mp")
    return dp, mp, dp // 2, lax.rem(dp, 2)


def partners(num_mp, num_z):
    dp, mp, z, core = place()
    pair = (z * 2 + 1 - core, mp)
    across = [lax.rem(mp + d, num_mp) for d in range(1, num_mp)]
    along = [lax.rem(z + d, num_z) for d in range(1, num_z)]
    return pair, [((dp, p), p) for p in across], [((p * 2 + core, mp), p) for p in along]


def meet(targets):
    barrier = pltpu.get_barrier_semaphore()
    for target in targets:
        pl.semaphore_signal(barrier, inc=1, device_id=target, device_id_type=MESH)
    pl.semaphore_wait(barrier, len(targets))


def sender(send_sem, recv_sem):
    count = [0]

    def send(source, landing, target):
        at = count[0]
        count[0] += 1
        copy = pltpu.make_async_remote_copy(
            src_ref=source,
            dst_ref=landing,
            send_sem=send_sem.at[at],
            recv_sem=recv_sem.at[at],
            device_id=target,
            device_id_type=MESH,
        )
        copy.start()
        return copy

    return send


def finish(copies):
    for copy in copies:
        copy.wait()


def total(slots):
    result = slots[0]
    for index in range(1, slots.shape[0]):
        result = result + slots[index]
    return result


def sum_gram(send, groups, part, pair_box, half, mp_box, z_box, full):
    pair, across, along = groups
    _, mp, z, core = place()
    half_rows, rows = half.shape[0], mp_box.shape[1]
    finish([send(part.at[rows_at(1 - core, half_rows)], pair_box, pair)])
    half[...] = part[rows_at(core, half_rows), :] + pair_box[...]
    copies = [send(half.at[rows_at(p, rows)], mp_box.at[mp], to) for to, p in across]
    mp_box[mp] = half[rows_at(mp, rows), :]
    finish(copies)
    z_box[z] = total(mp_box) * (1.0 / D)
    finish([send(z_box.at[z], z_box.at[z], to) for to, _ in along])
    own = rows_at(core * (half_rows // rows) + mp, rows)
    full[own, :] = total(z_box)
    finish([send(full.at[own], full.at[own], to) for to, _ in across])
    mine = rows_at(core, half_rows)
    finish([send(full.at[mine], full.at[mine], pair)])


def gram_scratch(n, num_mp, num_z):
    rows = n // 2 // num_mp
    shapes = [(n, n), (n // 2, n), (n // 2, n), (num_mp, rows, n), (num_z, rows, n), (n, n)]
    return [pltpu.VMEM(shape, jnp.float32) for shape in shapes]


def first_kernel(num_mp, num_z, part_ref, gram_ref, sum_ref, box, whole, *rest):
    *work, send_sem, recv_sem = rest
    groups = partners(num_mp, num_z)
    pair, across, along = groups
    _, mp, _, _ = place()
    send = sender(send_sem, recv_sem)
    chunk = box.shape[1]
    meet([pair] + [to for to, _ in across + along])
    copies = [send(part_ref.at[rows_at(p, chunk)], box.at[mp], to) for to, p in across]
    box[mp] = part_ref[rows_at(mp, chunk), :]
    finish(copies)
    own = rows_at(mp, chunk)
    mine = total(box)
    whole[own, :] = mine
    spread = [send(whole.at[own], whole.at[own], to) for to, _ in across]
    work[0][...] = dot(mine, mine, ((0,), (0,)))
    sum_gram(send, groups, *work)
    gram_ref[...] = work[-1][...]
    finish(spread)
    sum_ref[...] = whole[...]


def second_kernel(num_mp, num_z, part_ref, gram_ref, sum_ref, pair_sum, joined, box, *rest):
    *work, send_sem, recv_sem = rest
    groups = partners(num_mp, num_z)
    pair, across, along = groups
    _, _, z, core = place()
    send = sender(send_sem, recv_sem)
    half_rows, chunk = joined.shape[0], box.shape[1]
    meet([pair] + [to for to, _ in across + along])
    finish([send(part_ref.at[rows_at(1 - core, half_rows)], pair_sum, pair)])
    joined[...] = part_ref[rows_at(core, half_rows), :] + pair_sum[...]
    copies = [send(joined.at[rows_at(p, chunk)], box.at[z], to) for to, p in along]
    box[z] = joined[rows_at(z, chunk), :]
    finish(copies)
    mine = total(box)
    sum_ref[...] = mine
    work[0][...] = dot(mine, mine, ((0,), (0,)))
    sum_gram(send, groups, *work)
    gram_ref[...] = work[-1][...]


def swap_kernel(num_dp, part_ref, out_ref, box, send_sem, recv_sem):
    dp, mp, _, _ = place()
    width = box.shape[1]
    others = [lax.rem(dp + d, num_dp) for d in range(1, num_dp)]
    send = sender(send_sem, recv_sem)
    meet([(p, mp) for p in others])
    copies = [send(part_ref.at[rows_at(p, width)], box.at[dp], (p, mp)) for p in others]
    box[dp] = part_ref[rows_at(dp, width), :]
    finish(copies)
    out_ref[...] = box[...]


def remote_call(body, collective_id, outs, scratch, copies, value):
    vmem = pl.BlockSpec(memory_space=pltpu.VMEM)
    return pl.pallas_call(
        body,
        out_shape=[jax.ShapeDtypeStruct(shape, jnp.float32) for shape in outs],
        in_specs=[vmem],
        out_specs=[vmem] * len(outs),
        scratch_shapes=scratch
        + [pltpu.SemaphoreType.DMA((copies,)), pltpu.SemaphoreType.DMA((copies,))],
        compiler_params=pltpu.CompilerParams(
            collective_id=collective_id, has_side_effects=True, vmem_limit_bytes=48 * 2**20
        ),
    )(value)


def sum_first(part, num_mp, num_z):
    height, n = part.shape
    chunk = height // num_mp
    scratch = [
        pltpu.VMEM((num_mp, chunk, n), jnp.float32),
        pltpu.VMEM((height, n), jnp.float32),
    ] + gram_scratch(n, num_mp, num_z)
    copies = 4 * (num_mp - 1) + num_z - 1 + 2
    body = functools.partial(first_kernel, num_mp, num_z)
    return remote_call(body, 0, [(n, n), (height, n)], scratch, copies, part)


def sum_second(part, num_mp, num_z):
    height, n = part.shape
    chunk = height // 2 // num_z
    scratch = [
        pltpu.VMEM((height // 2, n), jnp.float32),
        pltpu.VMEM((height // 2, n), jnp.float32),
        pltpu.VMEM((num_z, chunk, n), jnp.float32),
    ] + gram_scratch(n, num_mp, num_z)
    copies = 2 * (num_mp - 1) + 2 * (num_z - 1) + 3
    body = functools.partial(second_kernel, num_mp, num_z)
    return remote_call(body, 1, [(n, n), (chunk, n)], scratch, copies, part)


def swap(part, num_dp):
    n, chunk = part.shape
    shape = (num_dp, n // num_dp, chunk)
    scratch = [pltpu.VMEM(shape, jnp.float32)]
    return remote_call(
        functools.partial(swap_kernel, num_dp), 2, [shape], scratch, num_dp - 1, part
    )[0]


def from_root(value, axis, root):
    mine = lax.axis_index(axis) == root
    return lax.psum(jnp.where(mine, value, jnp.zeros_like(value)), axis)


def body(grads, old_factor, basis):
    cols_here = old_factor.shape[1]
    num_mp = lax.axis_size("mp")
    num_dp = lax.axis_size("dp")
    num_z = num_dp // 2
    total_cols = grads.shape[1] * num_dp
    high = lax.Precision.HIGH
    basis_full = lax.all_gather(basis, "dp", axis=1, tiled=True)
    stripe_full = lax.all_gather(grads, "dp", axis=1, tiled=True)
    ratio = num_dp // num_mp
    offset = lax.axis_index("dp") % ratio * cols_here
    local_panel = lax.dynamic_slice_in_dim(stripe_full, offset, cols_here, 0)
    panel_full = from_root(local_panel, "mp", lax.axis_index("dp") // ratio)
    summed_block = lax.dot_general(
        stripe_full, panel_full, (((1,), (1,)), ((), ())), preferred_element_type=jnp.float32
    )
    new_factor = 0.95 * old_factor + 0.05 / total_cols * summed_block
    part_one = dot(new_factor, basis_full, ((0,), (0,)), high)
    gram_one, product_one = sum_first(part_one, num_mp, num_z)
    basis_one = dot(product_one, inverse_factor(gram_one), ((1,), (1,)))
    part_two = dot(new_factor, basis_one, ((1,), (0,)), high)
    gram_two, product_two = sum_second(part_two, num_mp, num_z)
    basis_two = dot(inverse_factor(gram_two), product_two, ((1,), (1,)))
    blocks = swap(basis_two, num_dp)
    blocks = blocks.reshape(num_z, 2, *blocks.shape[1:])
    new_basis = blocks.transpose(1, 0, 3, 2).reshape(basis.shape)
    return (new_factor, new_basis, basis_one)


def solution(mesh):
    placed = (P("mp", "dp"), P("mp", "dp"), P("mp", "dp"))
    return jax.shard_map(
        body,
        mesh=mesh,
        in_specs=placed,
        out_specs=(P("mp", "dp"), P("mp", "dp"), P("dp", None)),
        check_vma=False,
    )
```

time: 903 us -> 507 us (0.56)
  waiting for transfers between devices: 476 us -> 204 us
  other arithmetic: 258 us -> 5.47 us
  Pallas kernels: 0 us -> 224 us
  matrix products: 97 us -> 37.6 us
  local copies, waits for them, and re-layouts: 43.4 us -> 19.9 us
    psum x4 -> x0, waiting for transfers between devices: 263 us -> none  [the longest x1 95.6 us: body(): product_two = lax.psum(contract_last(basis_one, new_factor), 'dp')]
    another operation x34 -> x0, other arithmetic: 247 us -> none  [the longest x14 87.3 us: body(): lower_one = jnp.linalg.cholesky(gram_one)]
    pallas_call x0 -> x5, Pallas kernels: none -> 224 us  [the longest x3 174 us: remote_call(): pl.pallas_call(body, out_shape=[jax.ShapeDtypeStruct(shape, jnp.float32)...]
    dot_general x4, matrix products: 51.7 us -> 21.6 us  [dot(): lax.dot_general(left, right, (dims, ((), ())), precision=precision, prefe...]
    another operation x26 -> x0, matrix products: 29.4 us -> none  [the longest x7 11.1 us: body(): lax.linalg.triangular_solve(lower_two, product_two, left_side=True, lower...]
    another operation x33 -> x0, local copies, waits for them, and re-layouts: 20.5 us -> none
    all_gather x1, waiting for transfers between devices: 32.9 us -> 23.6 us  [body(): basis_full = lax.all_gather(basis, 'dp', axis=1, tiled=True)]
    unnamed x19 -> x6, local copies, waits for them, and re-layouts: 22.3 us -> 18.5 us
  transfers between devices with their start and end apart: 7 -> 3, of which waited for: 7 -> 3; matrix products, arithmetic and copies ran while one was open for 4% -> 7% of each run, Pallas kernels for 0% -> 0%
where the time goes in v1:
time: 507 us; the launch traced here: 505 us
  Pallas kernels  224 us (44%)
  waiting for transfers between devices  204 us (40%)
  matrix products  37.6 us (7%)
  local copies, waits for them, and re-layouts  19.9 us (4%)
  between operations  13.9 us (3%)
  other arithmetic  5.47 us (1%)
    pallas_call x3, Pallas kernels, remote_call(): pl.pallas_call(body, out_shape=[jax.ShapeDtypeStruct(shape, jnp.float32)...  174 us
    psum x1, waiting for transfers between devices, from_root(): return lax.psum(jnp.where(mine, value, jnp.zeros_like(value)), axis)  92.2 us
    all_gather x1, waiting for transfers between devices, body(): stripe_full = lax.all_gather(grads, 'dp', axis=1, tiled=True)  86.9 us
    pallas_call x2, Pallas kernels, inverse_factor(): pl.pallas_call(factor_kernel, out_shape=jax.ShapeDtypeStruct(gram.shape,...  50.7 us
    all_gather x1, waiting for transfers between devices, body(): basis_full = lax.all_gather(basis, 'dp', axis=1, tiled=True)  23.6 us
    dot_general x4, matrix products, dot(): lax.dot_general(left, right, (dims, ((), ())), precision=precision, prefe...  21.6 us
    unnamed x6, local copies, waits for them, and re-layouts  18.5 us
    dot_general x1, matrix products, body(): lax.dot_general(stripe_full, panel_full, (((1,), (1,)), ((), ())), prefer...  16 us
  transfers between devices with their start and end apart: 3, of which 3 were waited for; matrix products, arithmetic and copies ran while one was open for 7% of the time, Pallas kernels for 0%

profile of v1, /device:TPU:0, one launch (start us, length us, event | category | flops | bytes accessed | tf_op | source)
XLA Modules:
  0.0 505.3 jit_solution(1720140968841139302)
XLA Ops:
  7.2 0.0 all-gather.3.cloned.1.call-start
  7.2 0.7 all-gather.3.cloned.1.call-update
  7.9 0.0 all-reduce.2.cloned.1.call-start
  8.0 86.9 %all-gather.3.cloned.1.call-done = bf16[2048,2048]{1,0:T(8,128)(2,1)} async-done(((bf16[2048,256]{1,0:T(8,128)(2,1)}), bf16[2048,2048]{1,0:T(8,128)(2,1)}) %all-gather.3.cloned.1.call-update) | async-done | bytes 8388624 | tf_op jit(solution)/shard_map/all_gather | solution.py:282
  94.8 5.5 %dynamic-slice_select_fusion = bf16[1024,2048]{1,0:T(8,128)(2,1)} fusion(bf16[2048,2048]{1,0:T(8,128)(2,1)} %all-gather.3.cloned.1.call-done, s32[]{:T(128)S(6)} %select_n.25, pred[]{:T(512)S(6)} %eq.5), kind=kLoop, calls=%fused_computation.1 | loop fusion | flops 2097152 | bytes 8388613 | tf_op jit(solution)/shard_map/jit(_where)/select_n | solution.py:271
  100.3 0.0 all-reduce.2.cloned.1.call-update
  100.3 0.0 all-gather.5.cloned.1.call-start
  100.4 0.7 all-gather.5.cloned.1.call-update
  101.1 9.2 %copy.6 = f32[2048,1024]{0,1:T(8,128)} copy(f32[2048,1024]{1,0:T(8,128)} %param.4) | data formatting | bytes 16777216 | tf_op args[1]
  110.3 92.2 %all-reduce.2.cloned.1.call-done = bf16[1024,2048]{1,0:T(8,128)(2,1)} async-done(((bf16[1024,2048]{1,0:T(8,128)(2,1)}), bf16[1024,2048]{1,0:T(8,128)(2,1)}) %all-reduce.2.cloned.1.call-update) | async-done | bytes 4194320 | tf_op jit(solution)/shard_map/psum | solution.py:271
  202.5 16.0 %bitcast_add_fusion = f32[2048,1024]{0,1:T(8,128)} fusion(f32[2048,1024]{0,1:T(8,128)} %copy.6, bf16[1024,2048]{1,0:T(8,128)(2,1)} %all-reduce.2.cloned.1.call-done, bf16[2048,2048]{1,0:T(8,128)(2,1)} %all-gather.3.cloned.1.call-done), kind=kOutput, calls=%fused_computation | convolution fusion | flops 8596226048 | bytes 29360128 | tf_op jit(solution)/shard_map/dot_general | solution.py:287
  218.6 9.3 %copy.8 = f32[2048,1024]{1,0:T(8,128)} copy(f32[2048,1024]{0,1:T(8,128)} %bitcast_add_fusion) | data formatting | bytes 16777216
  227.8 23.6 %all-gather.5.cloned.1.call-done = f32[2048,512]{0,1:T(8,128)} async-done(((f32[2048,64]{0,1:T(8,128)}), f32[2048,512]{0,1:T(8,128)}) %all-gather.5.cloned.1.call-update) | async-done | bytes 4194320 | tf_op jit(solution)/shard_map/all_gather | solution.py:281
  251.4 10.4 %fusion.part_ref = f32[1024,512]{1,0:T(8,128)S(1)} fusion(f32[2048,1024]{0,1:T(8,128)} %bitcast_add_fusion, f32[2048,512]{0,1:T(8,128)} %all-gather.5.cloned.1.call-done), kind=kOutput, calls=%fused_computation.2 | convolution fusion | flops 6442450944 | bytes 14680064 | tf_op jit(solution)/shard_map/dot_general | solution.py:18
  261.8 0.0 copy-start
  261.8 75.7 %shard_map.58 = (f32[512,512]{1,0:T(8,128)S(1)}, f32[1024,512]{1,0:T(8,128)S(1)}) custom-call(f32[1024,512]{1,0:T(8,128)S(1)} %fusion.part_ref), custom_call_target="tpu_custom_call" | custom-call | tf_op jit(solution)/shard_map/pallas_call | solution.py:222
  337.5 25.4 %shard_map.59 = f32[512,512]{1,0:T(8,128)S(1)} custom-call(f32[512,512]{1,0:T(8,128)S(1)} %get-tuple-element.8.gram_ref), custom_call_target="tpu_custom_call" | custom-call | tf_op jit(solution)/shard_map/pallas_call | solution.py:76
  363.0 3.5 fusion.1
  366.4 0.0 copy-done
  366.4 0.0 copy-start.1
  366.5 6.7 %fusion.2.part_ref = f32[2048,512]{1,0:T(8,128)S(1)} fusion(f32[2048,1024]{0,1:T(8,128)S(1)} %copy-done, f32[1024,512]{1,0:T(8,128)S(1)} %fusion.1), kind=kOutput, calls=%fused_computation.4 | convolution fusion | flops 6442450944 | bytes 14680064 | tf_op jit(solution)/shard_map/dot_general | solution.py:18
  373.2 0.0 copy-done.1
  373.2 84.8 %shard_map.60 = (f32[512,512]{1,0:T(8,128)S(1)}, f32[256,512]{1,0:T(8,128)S(1)}) custom-call(f32[2048,512]{1,0:T(8,128)S(1)} %fusion.2.part_ref), custom_call_target="tpu_custom_call" | custom-call | tf_op jit(solution)/shard_map/pallas_call | solution.py:222
  458.0 25.3 %shard_map.61 = f32[512,512]{1,0:T(8,128)S(1)} custom-call(f32[512,512]{1,0:T(8,128)S(1)} %get-tuple-element.9.gram_ref), custom_call_target="tpu_custom_call" | custom-call | tf_op jit(solution)/shard_map/pallas_call | solution.py:76
  483.3 1.0 fusion.3.part_ref
  484.3 13.0 %shard_map.62 = f32[8,64,256]{2,1,0:T(8,128)S(1)} custom-call(f32[512,256]{1,0:T(8,128)S(1)} %fusion.3.part_ref), custom_call_target="tpu_custom_call" | custom-call | tf_op jit(solution)/shard_map/pallas_call | solution.py:222
  497.3 0.3 copy.7
  497.7 1.1 reshape.13
Async XLA Ops:
  7.2 87.7 %all-gather.3.cloned.1.call-start = ((), (), s32[]{:S(2)}) async-start(), calls=%async_computation | async-start | bytes 9437184 | tf_op jit(solution)/shard_map/all_gather | solution.py:282
  7.9 194.6 %all-reduce.2.cloned.1.call-start = ((), (), s32[]{:S(2)}) async-start(), calls=%async_computation.1 | async-start | bytes 8388608 | tf_op jit(solution)/shard_map/psum | solution.py:271
  100.3 151.1 %all-gather.5.cloned.1.call-start = ((), (), s32[]{:S(2)}) async-start(), calls=%async_computation.2 | async-start | bytes 4718592 | tf_op jit(solution)/shard_map/all_gather | solution.py:281
  261.8 104.6 %copy-start = (f32[2048,1024]{0,1:T(8,128)S(1)}, f32[2048,1024]{0,1:T(8,128)}, u32[]{:S(2)}) copy-start(f32[2048,1024]{0,1:T(8,128)} %bitcast_add_fusion) | copy-start | bytes 25165828
  366.4 6.7 %copy-start.1 = (f32[1024,512]{1,0:T(8,128)}, f32[1024,512]{1,0:T(8,128)S(1)}, u32[]{:S(2)}) copy-start(f32[1024,512]{1,0:T(8,128)S(1)} %fusion.1) | copy-start | bytes 6291460
Sparse Core Ops, SparseCore 0:
  9.6 85.1 all-gather.2
  100.4 102.0 all-reduce.1
  204.2 47.1 all-gather.4

commit v2 on v1

--- a/solution.py
+++ b/solution.py
@@ -266,9 +266,126 @@
     )[0]
 
 
-def from_root(value, axis, root):
-    mine = lax.axis_index(axis) == root
-    return lax.psum(jnp.where(mine, value, jnp.zeros_like(value)), axis)
+CHUNKS = 8
+
+
+def snake(index, side):
+    row, col = index // side, lax.rem(index, side)
+    return row * side + col + lax.rem(row, 2) * (side - 1 - 2 * col)
+
+
+def panel_kernel(num_dp, num_mp, side, stripe_ref, out_ref, panel, local_sem, send_sem, recv_sem):
+    dp, mp, _, _ = place()
+    ratio = num_dp // num_mp
+    height = panel.shape[0]
+    chunk = height // 2 // CHUNKS
+    at = snake(mp, side)
+    root = snake(dp // ratio, side)
+    after = (dp, snake(lax.rem(at + 1, num_mp), side))
+    before = (dp, snake(lax.rem(at + num_mp - 1, num_mp), side))
+    meet([after, before])
+    ways = (
+        (lax.rem(at - root + num_mp, num_mp), after),
+        (lax.rem(root - at + num_mp, num_mp), before),
+    )
+
+    @pl.when(at == root)
+    def _():
+        mine = stripe_ref.at[rows_at(lax.rem(dp, ratio), height)]
+        copy = pltpu.make_async_copy(mine, panel, local_sem)
+        copy.start()
+        copy.wait()
+
+    def piece(way, step):
+        rows = panel.at[pl.ds((way * CHUNKS + step) * chunk, chunk)]
+        return pltpu.make_async_remote_copy(
+            src_ref=rows,
+            dst_ref=rows,
+            send_sem=send_sem.at[way, step],
+            recv_sem=recv_sem.at[way, step],
+            device_id=ways[way][1],
+            device_id_type=MESH,
+        )
+
+    for step in range(CHUNKS):
+        for way in range(2):
+            pl.when(ways[way][0] > 0)(piece(way, step).wait_recv)
+            pl.when(ways[way][0] < num_mp - 1)(piece(way, step).start)
+    for way in range(2):
+        for step in range(CHUNKS):
+            pl.when(ways[way][0] < num_mp - 1)(piece(way, step).wait_send)
+    copy = pltpu.make_async_copy(panel, out_ref, local_sem)
+    copy.start()
+    copy.wait()
+
+
+def gather_panel(stripe, cols_here, num_dp, num_mp):
+    side = max(s for s in range(1, num_mp + 1) if s * s <= num_mp)
+    shape = (cols_here, stripe.shape[1])
+    return pl.pallas_call(
+        functools.partial(panel_kernel, num_dp, num_mp, side),
+        out_shape=jax.ShapeDtypeStruct(shape, stripe.dtype),
+        in_specs=[pl.BlockSpec(memory_space=pl.ANY)],
+        out_specs=pl.BlockSpec(memory_space=pl.ANY),
+        scratch_shapes=[
+            pltpu.VMEM(shape, stripe.dtype),
+            pltpu.SemaphoreType.DMA,
+            pltpu.SemaphoreType.DMA((2, CHUNKS)),
+            pltpu.SemaphoreType.DMA((2, CHUNKS)),
+        ],
+        compiler_params=pltpu.CompilerParams(
+            collective_id=3, has_side_effects=True, vmem_limit_bytes=48 * 2**20
+        ),
+        cost_estimate=pl.CostEstimate(flops=0, bytes_accessed=128 * 2**20, transcendentals=0),
+    )(stripe)
+
+
+def split(value):
+    top = value.astype(jnp.bfloat16)
+    return top, (value - top.astype(jnp.float32)).astype(jnp.bfloat16)
+
+
+def factor_step(scale, old_ref, stripe_ref, panel_ref, basis_ref, new_ref, part_ref):
+    height = old_ref.shape[0]
+    tall = min(height, 512)
+    inner = ((1,), (0,))
+    result = jnp.zeros(part_ref.shape[::-1], jnp.float32)
+    for start in range(0, height, tall):
+        rows = pl.ds(start, tall)
+        summed = dot(stripe_ref[rows, :], panel_ref[...], ((1,), (1,)), None)
+        value = 0.95 * old_ref[rows, :] + scale * summed
+        new_ref[rows, :] = value
+        top, low = split(value)
+        basis_top, basis_low = split(basis_ref[:, rows])
+        result += dot(basis_top, top, inner, None)
+        result += dot(basis_low, top, inner, None) + dot(basis_top, low, inner, None)
+    part_ref[...] = result.T
+
+
+def update_factor(old_factor, stripe, panel, basis_full):
+    height, width = old_factor.shape
+    depth, n = stripe.shape[1], basis_full.shape[0]
+    tile = 256
+    whole = lambda i: (0, 0)
+    return pl.pallas_call(
+        functools.partial(factor_step, 0.05 / depth),
+        grid=(width // tile,),
+        out_shape=[
+            jax.ShapeDtypeStruct((height, width), jnp.float32),
+            jax.ShapeDtypeStruct((width, n), jnp.float32),
+        ],
+        in_specs=[
+            pl.BlockSpec((height, tile), lambda i: (0, i)),
+            pl.BlockSpec((height, depth), whole, pipeline_mode=pl.Buffered(1)),
+            pl.BlockSpec((tile, depth), lambda i: (i, 0)),
+            pl.BlockSpec((n, height), whole, pipeline_mode=pl.Buffered(1)),
+        ],
+        out_specs=[
+            pl.BlockSpec((height, tile), lambda i: (0, i)),
+            pl.BlockSpec((tile, n), lambda i: (i, 0)),
+        ],
+        compiler_params=pltpu.CompilerParams(vmem_limit_bytes=48 * 2**20),
+    )(old_factor, stripe, panel, basis_full)
 
 
 def body(grads, old_factor, basis):
@@ -276,19 +393,12 @@
     num_mp = lax.axis_size("mp")
     num_dp = lax.axis_size("dp")
     num_z = num_dp // 2
-    total_cols = grads.shape[1] * num_dp
     high = lax.Precision.HIGH
-    basis_full = lax.all_gather(basis, "dp", axis=1, tiled=True)
     stripe_full = lax.all_gather(grads, "dp", axis=1, tiled=True)
-    ratio = num_dp // num_mp
-    offset = lax.axis_index("dp") % ratio * cols_here
-    local_panel = lax.dynamic_slice_in_dim(stripe_full, offset, cols_here, 0)
-    panel_full = from_root(local_panel, "mp", lax.axis_index("dp") // ratio)
-    summed_block = lax.dot_general(
-        stripe_full, panel_full, (((1,), (1,)), ((), ())), preferred_element_type=jnp.float32
-    )
-    new_factor = 0.95 * old_factor + 0.05 / total_cols * summed_block
-    part_one = dot(new_factor, basis_full, ((0,), (0,)), high)
+    basis_rows, stripe_full = lax.optimization_barrier((basis.T, stripe_full))
+    basis_full = lax.all_gather(basis_rows, "dp", axis=0, tiled=True)
+    panel_full = gather_panel(stripe_full, cols_here, num_dp, num_mp)
+    new_factor, part_one = update_factor(old_factor, stripe_full, panel_full, basis_full)
     gram_one, product_one = sum_first(part_one, num_mp, num_z)
     basis_one = dot(product_one, inverse_factor(gram_one), ((1,), (1,)))
     part_two = dot(new_factor, basis_one, ((1,), (0,)), high)

time: 507 us -> 566 us (1.12)
  Pallas kernels: 224 us -> 445 us
  waiting for transfers between devices: 204 us -> 87.6 us
  matrix products: 37.6 us -> 14.3 us
  local copies, waits for them, and re-layouts: 19.9 us -> 3.33 us
    pallas_call x3, Pallas kernels: 174 us -> 317 us  [remote_call(): pl.pallas_call(body, out_shape=[jax.ShapeDtypeStruct(shape, jnp.float32)...]
    psum x1 -> x0, waiting for transfers between devices: 92.2 us -> none  [from_root(): return lax.psum(jnp.where(mine, value, jnp.zeros_like(value)), axis)]
    pallas_call x0 -> x2, Pallas kernels: none -> 76.6 us  [the longest x1 49.6 us: gather_panel(): pl.pallas_call(functools.partial(panel_kernel, num_dp, num_mp, side), out...]
    all_gather x1, waiting for transfers between devices: 23.6 us -> 0.01 us  [body(): basis_full = lax.all_gather(basis_rows, 'dp', axis=0, tiled=True)]
    unnamed x6 -> x4, local copies, waits for them, and re-layouts: 18.5 us -> 1.93 us
    dot_general x1 -> x0, matrix products: 16 us -> none  [body(): lax.dot_general(stripe_full, panel_full, (((1,), (1,)), ((), ())), prefer...]
    dot_general x4 -> x3, matrix products: 21.6 us -> 14.3 us  [dot(): lax.dot_general(left, right, (dims, ((), ())), precision=precision, prefe...]
  transfers between devices with their start and end apart: 3 -> 2, of which waited for: 3 -> 1; matrix products, arithmetic and copies ran while one was open for 7% -> 0% of each run, Pallas kernels for 0% -> 9%
where the time goes in v2:
time: 566 us; the launch traced here: 564 us
  Pallas kernels  445 us (79%)
  waiting for transfers between devices  87.6 us (15%)
  matrix products  14.3 us (3%)
  between operations  14.1 us (2%)
    pallas_call x3, Pallas kernels, remote_call(): pl.pallas_call(body, out_shape=[jax.ShapeDtypeStruct(shape, jnp.float32)...  317 us
    all_gather x1, waiting for transfers between devices, body(): stripe_full = lax.all_gather(grads, 'dp', axis=1, tiled=True)  86.9 us
    pallas_call x2, Pallas kernels, inverse_factor(): pl.pallas_call(factor_kernel, out_shape=jax.ShapeDtypeStruct(gram.shape,...  50.9 us
    pallas_call x1, Pallas kernels, gather_panel(): pl.pallas_call(functools.partial(panel_kernel, num_dp, num_mp, side), out...  49.6 us
    pallas_call x1, Pallas kernels, update_factor(): pl.pallas_call(functools.partial(factor_step, 0.05 / depth), grid=(width...  27 us
    dot_general x3, matrix products, dot(): lax.dot_general(left, right, (dims, ((), ())), precision=precision, prefe...  14.3 us
  transfers between devices with their start and end apart: 2, of which 1 were waited for; matrix products, arithmetic and copies ran while one was open for 0% of the time, Pallas kernels for 9%

profile of v2, /device:TPU:0, one launch (start us, length us, event | category | flops | bytes accessed | tf_op | source)
XLA Modules:
  0.0 564.2 jit_solution(1280731055338591050)
XLA Ops:
  7.2 0.0 all-gather.3.cloned.1.call-start
  7.2 0.7 all-gather.3.cloned.1.call-update
  7.9 0.0 all-gather.5.cloned.1.call-start
  7.9 86.9 %all-gather.3.cloned.1.call-done.stripe_ref = bf16[2048,2048]{1,0:T(8,128)(2,1)} async-done(((bf16[2048,256]{1,0:T(8,128)(2,1)}), bf16[2048,2048]{1,0:T(8,128)(2,1)}) %all-gather.3.cloned.1.call-update) | async-done | bytes 8388624 | tf_op jit(solution)/shard_map/all_gather | solution.py:397
  94.8 0.0 all-gather.5.cloned.1.call-update
  94.8 49.6 %shard_map.58.panel_ref = bf16[1024,2048]{1,0:T(8,128)(2,1)S(1)} custom-call(bf16[2048,2048]{1,0:T(8,128)(2,1)} %all-gather.3.cloned.1.call-done.stripe_ref), custom_call_target="tpu_custom_call" | custom-call | bytes 134217728 | tf_op jit(solution)/shard_map/pallas_call | solution.py:325
  144.5 0.0 copy-start
  144.5 1.9 copy-done
  146.4 0.0 all-gather.5.cloned.1.call-done.basis_ref
  146.4 27.0 %shard_map.59 = (f32[2048,1024]{1,0:T(8,128)}, f32[1024,512]{1,0:T(8,128)S(1)}) custom-call(f32[2048,1024]{1,0:T(8,128)} %old_ref.1, bf16[2048,2048]{1,0:T(8,128)(2,1)} %all-gather.3.cloned.1.call-done.stripe_ref, bf16[1024,2048]{1,0:T(8,128)(2,1)} %copy-done, f32[512,2048]{1,0:T(8,128)} %all-gather.5.cloned.1.call-done.basis_ref), custom_call_target="tpu_custom_call" | custom-call | tf_op jit(solution)/shard_map/pallas_call | solution.py:370
  173.4 218.5 %shard_map.60 = (f32[512,512]{1,0:T(8,128)S(1)}, f32[1024,512]{1,0:T(8,128)S(1)}) custom-call(f32[1024,512]{1,0:T(8,128)S(1)} %get-tuple-element.14.part_ref), custom_call_target="tpu_custom_call" | custom-call | tf_op jit(solution)/shard_map/pallas_call | solution.py:222
  391.9 25.5 %shard_map.61 = f32[512,512]{1,0:T(8,128)S(1)} custom-call(f32[512,512]{1,0:T(8,128)S(1)} %get-tuple-element.16.gram_ref), custom_call_target="tpu_custom_call" | custom-call | tf_op jit(solution)/shard_map/pallas_call | solution.py:76
  417.4 3.5 fusion
  420.8 0.0 copy-start.1
  420.9 9.9 %fusion.1.part_ref = f32[2048,512]{1,0:T(8,128)S(1)} fusion(f32[2048,1024]{1,0:T(8,128)} %get-tuple-element.8, f32[1024,512]{1,0:T(8,128)S(1)} %fusion), kind=kOutput, calls=%fused_computation.1 | convolution fusion | flops 6442450944 | bytes 14680064 | tf_op jit(solution)/shard_map/dot_general | solution.py:18
  430.7 0.0 copy-done.1
  430.7 85.4 %shard_map.62 = (f32[512,512]{1,0:T(8,128)S(1)}, f32[256,512]{1,0:T(8,128)S(1)}) custom-call(f32[2048,512]{1,0:T(8,128)S(1)} %fusion.1.part_ref), custom_call_target="tpu_custom_call" | custom-call | tf_op jit(solution)/shard_map/pallas_call | solution.py:222
  516.2 25.5 %shard_map.63 = f32[512,512]{1,0:T(8,128)S(1)} custom-call(f32[512,512]{1,0:T(8,128)S(1)} %get-tuple-element.17.gram_ref), custom_call_target="tpu_custom_call" | custom-call | tf_op jit(solution)/shard_map/pallas_call | solution.py:76
  541.7 1.0 fusion.2.part_ref
  542.7 13.2 %shard_map.64 = f32[8,64,256]{2,1,0:T(8,128)S(1)} custom-call(f32[512,256]{1,0:T(8,128)S(1)} %fusion.2.part_ref), custom_call_target="tpu_custom_call" | custom-call | tf_op jit(solution)/shard_map/pallas_call | solution.py:222
  555.9 0.3 copy.6
  556.3 1.1 reshape.13
Async XLA Ops:
  7.2 87.7 %all-gather.3.cloned.1.call-start = ((), (), s32[]{:S(2)}) async-start(), calls=%async_computation | async-start | bytes 9437184 | tf_op jit(solution)/shard_map/all_gather | solution.py:397
  7.9 138.5 %all-gather.5.cloned.1.call-start = ((), (), s32[]{:S(2)}) async-start(), calls=%async_computation.1 | async-start | bytes 4718592 | tf_op jit(solution)/shard_map/all_gather | solution.py:399
  144.5 1.9 copy-start
  420.8 9.9 %copy-start.1 = (f32[1024,512]{1,0:T(8,128)}, f32[1024,512]{1,0:T(8,128)S(1)}, u32[]{:S(2)}) copy-start(f32[1024,512]{1,0:T(8,128)S(1)} %fusion) | copy-start | bytes 6291460
Sparse Core Ops, SparseCore 0:
  9.6 85.1 all-gather.2
  96.4 45.3 all-gather.4
